TPU v7x, 32 devices: a whole 2x2x4 slice. The times are simulated.
32 devices in a mesh: groups: 2 (over x), feat: 8 (over z, y), tok: 2 (over core).
Axes of the slice: x: 2, y: 2, z: 4, core: 2. Of those that a mesh axis runs over, the one named last changes fastest.
Arguments:
- activations: bfloat16 [16384, 2048], P(('groups', 'feat'), 'tok'), parts along dimension 0, may hold values from -6 to 6
Outputs:
- hessian: float32 [16384, 8192], P(('groups', 'feat'), 'tok'), parts along dimension 0
There are 2 independent parts, one for each index of `groups`. A program takes and returns all parts, laid end to end along the dimension named above; each array names one. Nothing has to cross between parts.
All inputs are finite; a program needn't handle non-finite values.
Results may differ from a plain program's by a relative error of at most 0.0003.
Values may be sent and summed in bfloat16 or wider, within the bound.
A program may use at most 192 MiB of HBM per device.

v0:
```python
import jax
import jax.numpy as jnp
from jax import lax
from jax.sharding import PartitionSpec as P


def shards(activations):
    tok_count = lax.axis_size("tok")
    factor = 2.0 / (activations.shape[1] * tok_count)
    tile_block = jnp.einsum(
        "ft,gt->fg",
        activations,
        lax.all_gather(activations, "feat", axis=0, tiled=True),
        preferred_element_type=jnp.float32,
    )
    return lax.psum_scatter(tile_block, "tok", scatter_dimension=1, tiled=True) * factor


def solution(mesh):
    in_specs = (P(("groups", "feat"), "tok"),)
    out_specs = P(("groups", "feat"), "tok")
    return jax.shard_map(shards, mesh=mesh, in_specs=in_specs, out_specs=out_specs, check_vma=False)
```

profile of v0, /device:TPU:1, one launch (start us, length us, event | category | flops | bytes accessed | tf_op | source)
XLA Modules:
  0.0 327.6 jit_solution(7532965638772700786)
XLA Ops:
  6.5 0.0 all-gather.2.cloned.1.call-start
  6.5 0.7 all-gather.2.cloned.1.call-update
  7.3 0.0 reduce-scatter.2.cloned.1.call-start
  7.3 231.5 %all-gather.2.cloned.1.call-done = bf16[8192,1024]{1,0:T(8,128)(2,1)} async-done(((bf16[1024,1024]{1,0:T(8,128)(2,1)}), bf16[8192,1024]{1,0:T(8,128)(2,1)}) %all-gather.2.cloned.1.call-update) | async-done | bytes 16777232 | tf_op jit(solution)/shard_map/all_gather | solution.py:13
  238.8 25.8 %fusion = f32[1024,8192]{1,0:T(8,128)} fusion(bf16[1024,1024]{1,0:T(8,128)(2,1)} %param.1, bf16[8192,1024]{1,0:T(8,128)(2,1)} %all-gather.2.cloned.1.call-done), kind=kOutput, calls=%fused_computation.1 | convolution fusion | flops 17179869184 | bytes 52428800 | tf_op jit(solution)/shard_map/ft,gt->fg/dot_general | solution.py:10
  264.6 0.0 reduce-scatter.2.cloned.1.call-update
  264.7 44.3 %reduce-scatter.2.cloned.1.call-done = f32[1024,4096]{1,0:T(8,128)} async-done(((f32[1024,8192]{1,0:T(8,128)}), f32[1024,4096]{1,0:T(8,128)}) %reduce-scatter.2.cloned.1.call-update) | async-done | bytes 16777232 | tf_op jit(solution)/shard_map/reduce_scatter | solution.py:16
  309.0 11.7 %broadcast_multiply_fusion = f32[1024,4096]{1,0:T(8,128)} fusion(f32[1024,4096]{1,0:T(8,128)} %reduce-scatter.2.cloned.1.call-done), kind=kLoop, calls=%fused_computation | loop fusion | flops 4194304 | bytes 33554432 | tf_op jit(solution)/shard_map/mul | solution.py:16
Async XLA Ops:
  6.5 232.3 %all-gather.2.cloned.1.call-start = ((), (), s32[]{:S(2)}) async-start(), calls=%async_computation.1 | async-start | bytes 18874368 | tf_op jit(solution)/shard_map/all_gather | solution.py:13
  7.3 301.7 %reduce-scatter.2.cloned.1.call-start = ((), (), s32[]{:S(2)}) async-start(), calls=%async_computation.2 | async-start | bytes 50331648 | tf_op jit(solution)/shard_map/reduce_scatter | solution.py:16
Sparse Core Ops, SparseCore 0:
  9.5 229.2 all-gather.1
  264.8 44.1 reduce-scatter.1
where the time goes:
time: 328 us
  waiting for transfers between devices  277 us (84%)
  matrix products  25.8 us (8%)
  between operations  13.4 us (4%)
  other arithmetic  11.7 us (4%)
    all_gather x1, waiting for transfers between devices, shards(): lax.all_gather(activations, 'feat', axis=0, tiled=True)  232 us
    reduce_scatter x1, waiting for transfers between devices, shards(): lax.psum_scatter(tile_block, 'tok', scatter_dimension=1, tiled=True)  44.3 us
    dot_general x1, matrix products, shards(): jnp.einsum('ft,gt->fg', activations, lax.all_gather(activations, 'feat',...  25.8 us
    mul x1, other arithmetic, shards(): lax.psum_scatter(tile_block, 'tok', scatter_dimension=1, tiled=True)  11.7 us
  transfers between devices with their start and end apart: 2, of which 2 were waited for; matrix products, arithmetic and copies ran while one was open for 0% of the time, Pallas kernels for 0%

commit v1 on v0

v1 whole, which is shorter than its diff:
```python
import functools

import jax
import jax.numpy as jnp
from jax import lax
from jax.experimental import pallas as pl
from jax.experimental.pallas import tpu as pltpu
from jax.sharding import PartitionSpec as P

MESH = pl.DeviceIdType.MESH
CHUNK = 64
TILE = 256
SHIFTED = 3
WINDOW = 3
LAG = 4


def kernel(planes, ys, cores, x_ref, o_ref, panels, sib, mate, stage,
           in_sem, out_sem, recv, sib_recv, mate_send, mate_recv, link_send, sib_send):
    n, rows, _ = panels.shape
    per = n // cores
    chunks = rows // CHUNK
    group = TILE // CHUNK
    shifted = SHIFTED if ys > 1 else 0
    ring = ys == 1
    factor = 2.0 / (panels.shape[2] * cores)

    me = lax.axis_index("feat")
    core = lax.axis_index("tok")
    z, y = me // ys, me % ys

    def at(plane, col):
        return lax.rem(plane + planes, planes) * ys + col

    def select(flag, a, b):
        return tuple(jnp.where(flag, i, j) for i, j in zip(a, b))

    if ring:
        counts = {1: (planes // 2,) * 2, -1: (planes - 1 - planes // 2,) * 2}
        most = planes // 2
    else:
        counts = {
            1: (planes - 1 - z, jnp.where(z > 0, planes - z, 0)),
            -1: (z, jnp.where(z < planes - 1, z + 1, 0)),
        }
        most = planes - 1

    def z_item(sign, first, count, t):
        t1 = jnp.maximum(t, 0)
        a = (at(z + sign * (first + t1 // chunks), y), t1 % chunks)
        if shifted:
            t2 = jnp.maximum(t - count * chunks, 0)
            b = (at(z + sign * (first + t2 // shifted), 1 - y), t2 % shifted)
            a = select(t < count * chunks, a, b)
        return (t >= 0) & (t < count * (chunks + shifted)), a[0], a[1]

    def y_item(col, t):
        rest = chunks - shifted
        v = jnp.maximum(t - chunks, 0)
        turn = jnp.where(z < planes // 2, 1, -1)
        far = (at(z + turn * (1 + v // rest), col), shifted + v % rest)
        i, c = select(t < chunks, (at(z, col), jnp.maximum(t, 0)), far)
        return (t >= 0) & (t < chunks + (planes - 1) * rest), i, c

    def sends(link, t):
        return y_item(y, t) if link == 2 else z_item((1, -1)[link], 0, counts[(1, -1)[link]][1], t)

    def arrivals(link, t):
        return y_item(1 - y, t) if link == 2 else z_item((1, -1)[link], 1, counts[(1, -1)[link]][0], t)

    links = (0, 1, 2) if ys > 1 else (0, 1)
    target = (at(z - 1, y), at(z + 1, y), at(z, 1 - y))

    def piece(i, c):
        return panels.at[i, pl.ds(pl.multiple_of(c * CHUNK, CHUNK), CHUNK)]

    def link_copy(link, t, i, c):
        return pltpu.make_async_remote_copy(
            piece(i, c), piece(i, c), link_send.at[link, t % WINDOW], recv.at[i, c],
            device_id={"feat": target[link]}, device_id_type=MESH)

    def sib_copy(link, t, i, c):
        there = sib.at[i % per, pl.ds(pl.multiple_of(c * CHUNK, CHUNK), CHUNK)]
        return pltpu.make_async_remote_copy(
            piece(i, c), there, sib_send.at[link, t % WINDOW], sib_recv.at[i % per, c],
            device_id={"tok": 1 - core}, device_id_type=MESH)

    def mate_copy():
        return pltpu.make_async_remote_copy(
            panels.at[me], mate, mate_send, mate_recv,
            device_id={"tok": 1 - core}, device_id_type=MESH)

    def mine(i):
        return i // per == core

    def tile(i, g, own):
        cols = pl.ds(pl.multiple_of(g * TILE, TILE), TILE)
        if not own:
            for q in range(group):
                sib_copy(0, 0, i, g * group + q).wait_recv()
        other = mate.at[cols] if own else sib.at[i % per, cols]
        a, b = panels[i, cols], other[...]

        @pl.loop(0, rows // TILE)
        def _(r):
            block = pl.ds(pl.multiple_of(r * TILE, TILE), TILE)
            nt = (((1,), (1,)), ((), ()))
            total = lax.dot_general(panels[me, block], a, nt, preferred_element_type=jnp.float32)
            total += lax.dot_general(mate[block], b, nt, preferred_element_type=jnp.float32)
            stage[block] = total * factor

        out = pl.ds(pl.multiple_of((i % per) * rows + g * TILE, TILE), TILE)
        copy = pltpu.make_async_copy(stage, o_ref.at[:, out], out_sem)
        copy.start()
        copy.wait()

    load = pltpu.make_async_copy(x_ref, panels.at[me], in_sem)
    load.start()
    barrier = pltpu.get_barrier_semaphore()
    pl.semaphore_signal(barrier, inc=1, device_id={"tok": 1 - core}, device_id_type=MESH)
    greeted = 1
    for link in links:
        if ring or link == 2:
            pl.semaphore_signal(barrier, inc=1, device_id={"feat": target[link]}, device_id_type=MESH)
            greeted = greeted + 1
        else:
            there = (z > 0, z < planes - 1)[link]

            @pl.when(there)
            def _():
                pl.semaphore_signal(barrier, inc=1, device_id={"feat": target[link]}, device_id_type=MESH)

            greeted = greeted + there.astype(jnp.int32)
    load.wait()
    pl.semaphore_wait(barrier, greeted)

    steps = most * (chunks + shifted)
    if ys > 1:
        steps = max(steps, chunks + (planes - 1) * (chunks - shifted))

    @pl.loop(0, steps + LAG + WINDOW)
    def _(s):
        for link in links:
            past, i, c = sends(link, s - WINDOW)

            @pl.when(past)
            def _():
                link_copy(link, s, i, c).wait_send()

            now, i, c = sends(link, s)

            @pl.when(now)
            def _():
                link_copy(link, s, i, c).start()

        @pl.when(s == 0)
        def _():
            mate_copy().start()

        @pl.when(s == LAG)
        def _():
            mate_copy().wait()

        for link in links:
            past, i, c = arrivals(link, s - LAG - WINDOW)

            @pl.when(past & ~mine(i))
            def _():
                sib_copy(link, s, i, c).wait_send()

            now, i, c = arrivals(link, s - LAG)

            @pl.when(now)
            def _():
                link_copy(link, 0, i, c).wait_recv()

            @pl.when(now & ~mine(i))
            def _():
                sib_copy(link, s, i, c).start()

        own_group = s - 2 * LAG

        @pl.when((own_group >= 0) & (own_group < rows // TILE) & mine(me))
        def _():
            tile(me, own_group, True)

        for link in links:
            now, i, c = arrivals(link, s - LAG)
            ready = now & mine(i) & (c % group == group - 1)
            if shifted:
                whole = (i % ys == y) | (i // ys == z) | (c // group * group >= shifted)
                ready = ready & whole

            @pl.when(ready)
            def _():
                tile(i, c // group, False)

    if shifted:
        @pl.loop(0, planes)
        def _(k):
            i = k * ys + 1 - y

            @pl.when(mine(i) & (k != z))
            def _():
                for g in range(pl.cdiv(shifted, group)):
                    tile(i, g, False)


def shards(planes, ys, cores, activations):
    rows, depth = activations.shape
    n = planes * ys
    per = n // cores
    chunks = rows // CHUNK
    dma = pltpu.SemaphoreType.DMA
    return pl.pallas_call(
        functools.partial(kernel, planes, ys, cores),
        out_shape=jax.ShapeDtypeStruct((rows, per * rows), jnp.float32),
        in_specs=[pl.BlockSpec(memory_space=pl.ANY)],
        out_specs=pl.BlockSpec(memory_space=pl.ANY),
        scratch_shapes=[
            pltpu.VMEM((n, rows, depth), jnp.bfloat16),
            pltpu.VMEM((per, rows, depth), jnp.bfloat16),
            pltpu.VMEM((rows, depth), jnp.bfloat16),
            pltpu.VMEM((rows, TILE), jnp.float32),
            dma, dma, dma((n, chunks)), dma((per, chunks)), dma, dma,
            dma((3, WINDOW)), dma((3, WINDOW)),
        ],
        compiler_params=pltpu.CompilerParams(
            collective_id=0, has_side_effects=True, vmem_limit_bytes=40 * 2**20),
        cost_estimate=pl.CostEstimate(
            flops=2 * rows * per * rows * depth * cores,
            bytes_accessed=4 * rows * per * rows, transcendentals=0),
    )(activations)


def solution(mesh):
    n, cores = mesh.shape["feat"], mesh.shape["tok"]
    ys = 2 if n == 8 else 1
    spec = P(("groups", "feat"), "tok")
    return jax.shard_map(
        functools.partial(shards, n // ys, ys, cores),
        mesh=mesh, in_specs=(spec,), out_specs=spec, check_vma=False)
```

time: 328 us -> 188 us (0.57)
  waiting for transfers between devices: 277 us -> 0 us
  Pallas kernels: 0 us -> 175 us
  matrix products: 25.8 us -> 0 us
  between operations: 13.4 us -> 0.01 us
  local copies, waits for them, and re-layouts: 0 us -> 13.3 us
  other arithmetic: 11.7 us -> 0 us
    all_gather x1 -> x0, waiting for transfers between devices: 232 us -> none  [shards(): lax.all_gather(activations, 'feat', axis=0, tiled=True)]
    pallas_call x0 -> x1, Pallas kernels: none -> 175 us  [shards(): pl.pallas_call(functools.partial(kernel, planes, ys, cores), out_shape=ja...]
    reduce_scatter x1 -> x0, waiting for transfers between devices: 44.3 us -> none  [shards(): lax.psum_scatter(tile_block, 'tok', scatter_dimension=1, tiled=True)]
    dot_general x1 -> x0, matrix products: 25.8 us -> none  [shards(): jnp.einsum('ft,gt->fg', activations, lax.all_gather(activations, 'feat',...]
    unnamed x0 -> x3, local copies, waits for them, and re-layouts: none -> 13.3 us
    mul x1 -> x0, other arithmetic: 11.7 us -> none  [shards(): lax.psum_scatter(tile_block, 'tok', scatter_dimension=1, tiled=True)]
  transfers between devices with their start and end apart: 2 -> 0, of which waited for: 2 -> 0; matrix products, arithmetic and copies ran while one was open for 0% -> 0% of each run, Pallas kernels for 0% -> 0%
where the time goes in v1:
time: 188 us
  Pallas kernels  175 us (93%)
  local copies, waits for them, and re-layouts  13.3 us (7%)
    pallas_call x1, Pallas kernels, shards(): pl.pallas_call(functools.partial(kernel, planes, ys, cores), out_shape=ja...  175 us
    unnamed x3, local copies, waits for them, and re-layouts  13.3 us

profile of v1, /device:TPU:1, one launch (start us, length us, event | category | flops | bytes accessed | tf_op | source)
XLA Modules:
  0.0 188.2 jit_solution(13820191309769689797)
XLA Ops:
  0.0 0.0 copy-start
  0.0 1.6 copy-done
  1.6 174.8 %shard_map.17 = f32[1024,4096]{1,0:T(8,128)} custom-call(bf16[1024,1024]{1,0:T(8,128)(2,1)S(1)} %copy-done), custom_call_target="tpu_custom_call" | custom-call | flops 17179869184 | bytes 16777216 | tf_op jit(solution)/shard_map/pallas_call | solution.py:215
  176.4 11.7 %copy.3 = f32[1024,4096]{1,0:T(8,128)} copy(f32[1024,4096]{1,0:T(8,128)} %shard_map.17) | data formatting | bytes 33554432
Async XLA Ops:
  0.0 1.6 copy-start

commit v2 on v1

--- a/solution.py
+++ b/solution.py
@@ -15,8 +15,8 @@
 LAG = 4
 
 
-def kernel(planes, ys, cores, x_ref, o_ref, panels, sib, mate, stage,
-           in_sem, out_sem, recv, sib_recv, mate_send, mate_recv, link_send, sib_send):
+def kernel(planes, ys, cores, x_ref, o_ref, panels, sib, mate,
+           in_sem, recv, sib_recv, mate_send, mate_recv, link_send, sib_send):
     n, rows, _ = panels.shape
     per = n // cores
     chunks = rows // CHUNK
@@ -45,6 +45,16 @@
         }
         most = planes - 1
 
+    def z_length(count):
+        short = jnp.where(count == planes - 1, 1, 0) if shifted else 0
+        return count * (chunks + shifted) - short
+
+    rest = chunks - shifted
+    y_regular = chunks + (planes - 1) * rest
+    turn = jnp.where(z < planes // 2, 1, -1)
+    at_end = (z == 0) | (z == planes - 1)
+    y_length = y_regular + at_end.astype(jnp.int32)
+
     def z_item(sign, first, count, t):
         t1 = jnp.maximum(t, 0)
         a = (at(z + sign * (first + t1 // chunks), y), t1 % chunks)
@@ -52,15 +62,14 @@
             t2 = jnp.maximum(t - count * chunks, 0)
             b = (at(z + sign * (first + t2 // shifted), 1 - y), t2 % shifted)
             a = select(t < count * chunks, a, b)
-        return (t >= 0) & (t < count * (chunks + shifted)), a[0], a[1]
+        return (t >= 0) & (t < z_length(count)), a[0], a[1]
 
     def y_item(col, t):
-        rest = chunks - shifted
         v = jnp.maximum(t - chunks, 0)
-        turn = jnp.where(z < planes // 2, 1, -1)
         far = (at(z + turn * (1 + v // rest), col), shifted + v % rest)
+        far = select(t < y_regular, far, (at(z - turn, col), shifted - 1))
         i, c = select(t < chunks, (at(z, col), jnp.maximum(t, 0)), far)
-        return (t >= 0) & (t < chunks + (planes - 1) * rest), i, c
+        return (t >= 0) & (t < y_length), i, c
 
     def sends(link, t):
         return y_item(y, t) if link == 2 else z_item((1, -1)[link], 0, counts[(1, -1)[link]][1], t)
@@ -100,6 +109,7 @@
                 sib_copy(0, 0, i, g * group + q).wait_recv()
         other = mate.at[cols] if own else sib.at[i % per, cols]
         a, b = panels[i, cols], other[...]
+        out = pl.ds(pl.multiple_of((i % per) * rows + g * TILE, TILE), TILE)
 
         @pl.loop(0, rows // TILE)
         def _(r):
@@ -107,12 +117,7 @@
             nt = (((1,), (1,)), ((), ()))
             total = lax.dot_general(panels[me, block], a, nt, preferred_element_type=jnp.float32)
             total += lax.dot_general(mate[block], b, nt, preferred_element_type=jnp.float32)
-            stage[block] = total * factor
-
-        out = pl.ds(pl.multiple_of((i % per) * rows + g * TILE, TILE), TILE)
-        copy = pltpu.make_async_copy(stage, o_ref.at[:, out], out_sem)
-        copy.start()
-        copy.wait()
+            o_ref[block, out] = total * factor
 
     load = pltpu.make_async_copy(x_ref, panels.at[me], in_sem)
     load.start()
@@ -136,7 +141,7 @@
 
     steps = most * (chunks + shifted)
     if ys > 1:
-        steps = max(steps, chunks + (planes - 1) * (chunks - shifted))
+        steps = max(steps - 1, y_regular + 1)
 
     @pl.loop(0, steps + LAG + WINDOW)
     def _(s):
@@ -195,15 +200,18 @@
             def _():
                 tile(i, c // group, False)
 
-    if shifted:
-        @pl.loop(0, planes)
-        def _(k):
-            i = k * ys + 1 - y
-
-            @pl.when(mine(i) & (k != z))
-            def _():
-                for g in range(pl.cdiv(shifted, group)):
-                    tile(i, g, False)
+        for p in range(planes // cores if shifted else 0):
+            k = core * (planes // cores) + p
+            away = jnp.abs(k - z)
+            count = jnp.where(k > z, counts[1][0], counts[-1][0])
+            by_z = jnp.minimum(count * chunks + away * shifted, z_length(count)) - 1
+            turns = lax.rem((k - z) * turn + planes, planes) - 1
+            by_y = chunks + turns * rest + group - 1 - shifted
+            by_y = jnp.where(away == planes - 1, y_length - 1, by_y)
+
+            @pl.when((k != z) & (s - LAG == jnp.maximum(by_z, by_y)))
+            def _():
+                tile(k * ys + 1 - y, 0, False)
 
 
 def shards(planes, ys, cores, activations):
@@ -214,23 +222,22 @@
     dma = pltpu.SemaphoreType.DMA
     return pl.pallas_call(
         functools.partial(kernel, planes, ys, cores),
-        out_shape=jax.ShapeDtypeStruct((rows, per * rows), jnp.float32),
-        in_specs=[pl.BlockSpec(memory_space=pl.ANY)],
-        out_specs=pl.BlockSpec(memory_space=pl.ANY),
+        out_shape=pltpu.VMEM((rows, per * rows), jnp.float32),
+        in_specs=[pl.BlockSpec(memory_space=pltpu.HBM)],
+        out_specs=pl.BlockSpec(memory_space=pltpu.VMEM),
         scratch_shapes=[
             pltpu.VMEM((n, rows, depth), jnp.bfloat16),
             pltpu.VMEM((per, rows, depth), jnp.bfloat16),
             pltpu.VMEM((rows, depth), jnp.bfloat16),
-            pltpu.VMEM((rows, TILE), jnp.float32),
-            dma, dma, dma((n, chunks)), dma((per, chunks)), dma, dma,
+            dma, dma((n, chunks)), dma((per, chunks)), dma, dma,
             dma((3, WINDOW)), dma((3, WINDOW)),
         ],
         compiler_params=pltpu.CompilerParams(
-            collective_id=0, has_side_effects=True, vmem_limit_bytes=40 * 2**20),
+            collective_id=0, has_side_effects=True, vmem_limit_bytes=32 * 2**20),
         cost_estimate=pl.CostEstimate(
             flops=2 * rows * per * rows * depth * cores,
             bytes_accessed=4 * rows * per * rows, transcendentals=0),
-    )(activations)
+    )(pltpu.with_memory_space_constraint(activations, pltpu.HBM))
 
 
 def solution(mesh):

time: 188 us -> 176 us (0.936)
  local copies, waits for them, and re-layouts: 13.3 us -> 6.16 us
  Pallas kernels: 175 us -> 169 us
    unnamed x3 -> x1, local copies, waits for them, and re-layouts: 13.3 us -> 6.16 us
    pallas_call x1, Pallas kernels: 175 us -> 169 us  [shards(): pl.pallas_call(functools.partial(kernel, planes, ys, cores), out_shape=pl...]
where the time goes in v2:
time: 176 us
  Pallas kernels  169 us (96%)
  local copies, waits for them, and re-layouts  6.16 us (4%)
    pallas_call x1, Pallas kernels, shards(): pl.pallas_call(functools.partial(kernel, planes, ys, cores), out_shape=pl...  169 us
    unnamed x1, local copies, waits for them, and re-layouts  6.16 us

profile of v2, /device:TPU:1, one launch (start us, length us, event | category | flops | bytes accessed | tf_op | source)
XLA Modules:
  0.0 175.6 jit_solution(5326844348320518120)
XLA Ops:
  0.0 169.4 %shard_map.17 = f32[1024,4096]{1,0:T(8,128)S(1)} custom-call(bf16[1024,1024]{1,0:T(8,128)(2,1)} %x_ref.1), custom_call_target="tpu_custom_call" | custom-call | flops 17179869184 | bytes 16777216 | tf_op jit(solution)/shard_map/pallas_call | solution.py:223
  169.4 6.2 %copy.3 = f32[1024,4096]{1,0:T(8,128)} copy(f32[1024,4096]{1,0:T(8,128)S(1)} %shard_map.17) | data formatting | bytes 33554432

commit v3 on v2

--- a/solution.py
+++ b/solution.py
@@ -12,7 +12,7 @@
 TILE = 256
 SHIFTED = 3
 WINDOW = 3
-LAG = 4
+LAG = 3
 
 
 def kernel(planes, ys, cores, x_ref, o_ref, panels, sib, mate,
@@ -143,7 +143,7 @@
     if ys > 1:
         steps = max(steps - 1, y_regular + 1)
 
-    @pl.loop(0, steps + LAG + WINDOW)
+    @pl.loop(0, steps + max(LAG + 1, WINDOW))
     def _(s):
         for link in links:
             past, i, c = sends(link, s - WINDOW)
@@ -167,11 +167,11 @@
             mate_copy().wait()
 
         for link in links:
-            past, i, c = arrivals(link, s - LAG - WINDOW)
+            past, i, c = arrivals(link, s - LAG - 1)
 
             @pl.when(past & ~mine(i))
             def _():
-                sib_copy(link, s, i, c).wait_send()
+                sib_copy(link, s - 1, i, c).wait_send()
 
             now, i, c = arrivals(link, s - LAG)
 

time: 176 us -> 174 us (0.989)
  no operation moved by 1% of the time
where the time goes in v3:
time: 174 us
  Pallas kernels  168 us (97%)
  local copies, waits for them, and re-layouts  6.16 us (4%)
    pallas_call x1, Pallas kernels, shards(): pl.pallas_call(functools.partial(kernel, planes, ys, cores), out_shape=pl...  168 us
    unnamed x1, local copies, waits for them, and re-layouts  6.16 us

profile of v3, /device:TPU:1, one launch (start us, length us, event | category | flops | bytes accessed | tf_op | source)
XLA Modules:
  0.0 173.9 jit_solution(16338648114681822176)
XLA Ops:
  0.0 167.7 %shard_map.17 = f32[1024,4096]{1,0:T(8,128)S(1)} custom-call(bf16[1024,1024]{1,0:T(8,128)(2,1)} %x_ref.1), custom_call_target="tpu_custom_call" | custom-call | flops 17179869184 | bytes 16777216 | tf_op jit(solution)/shard_map/pallas_call | solution.py:223
  167.7 6.2 %copy.3 = f32[1024,4096]{1,0:T(8,128)} copy(f32[1024,4096]{1,0:T(8,128)S(1)} %shard_map.17) | data formatting | bytes 33554432

commit v4 on v3

--- a/solution.py
+++ b/solution.py
@@ -10,6 +10,7 @@
 MESH = pl.DeviceIdType.MESH
 CHUNK = 64
 TILE = 256
+BLOCK = 512
 SHIFTED = 3
 WINDOW = 3
 LAG = 3
@@ -111,9 +112,9 @@
         a, b = panels[i, cols], other[...]
         out = pl.ds(pl.multiple_of((i % per) * rows + g * TILE, TILE), TILE)
 
-        @pl.loop(0, rows // TILE)
+        @pl.loop(0, rows // BLOCK)
         def _(r):
-            block = pl.ds(pl.multiple_of(r * TILE, TILE), TILE)
+            block = pl.ds(pl.multiple_of(r * BLOCK, BLOCK), BLOCK)
             nt = (((1,), (1,)), ((), ()))
             total = lax.dot_general(panels[me, block], a, nt, preferred_element_type=jnp.float32)
             total += lax.dot_general(mate[block], b, nt, preferred_element_type=jnp.float32)

time: 174 us -> 174 us (level)
  no operation moved by 1% of the time
where the time goes in v4:
time: 174 us
  Pallas kernels  168 us (97%)
  local copies, waits for them, and re-layouts  6.16 us (4%)
    pallas_call x1, Pallas kernels, shards(): pl.pallas_call(functools.partial(kernel, planes, ys, cores), out_shape=pl...  168 us
    unnamed x1, local copies, waits for them, and re-layouts  6.16 us

profile of v4, /device:TPU:1, one launch (start us, length us, event | category | flops | bytes accessed | tf_op | source)
XLA Modules:
  0.0 173.7 jit_solution(11419174263475613498)
XLA Ops:
  0.0 167.6 %shard_map.17 = f32[1024,4096]{1,0:T(8,128)S(1)} custom-call(bf16[1024,1024]{1,0:T(8,128)(2,1)} %x_ref.1), custom_call_target="tpu_custom_call" | custom-call | flops 17179869184 | bytes 16777216 | tf_op jit(solution)/shard_map/pallas_call | solution.py:224
  167.6 6.2 %copy.3 = f32[1024,4096]{1,0:T(8,128)} copy(f32[1024,4096]{1,0:T(8,128)S(1)} %shard_map.17) | data formatting | bytes 33554432
